TPU v7x, 256 devices: a whole 4x4x8 slice. The times are simulated.
256 devices in a mesh: band: 4 (over z_hi, core), sx: 4 (over x), sy: 16 (over y, z_lo).
Axes of the slice: x: 4, y: 4, z: 8 (z_hi: 2, z_lo: 4; z = z_hi * 4 + z_lo), core: 2. Of those that a mesh axis runs over, the one named last changes fastest.
Arguments:
- orbitals: float32 [256, 24, 96, 128], P('band', 'sx', 'sy'), may hold values from -6 to 6
- potential: float32 [24, 96, 128], P('sx', 'sy'), may hold values from -3 to 0
- projectors: float32 [256, 4, 5, 128], P(('sx', 'sy')), may hold values from -0.25 to 0.25
- energies: float32 [256, 4], P(('sx', 'sy')), may hold values from 1 to 6
- centers: int32 [256, 2], P(('sx', 'sy')), may hold values from 0 to 95, as said below
Outputs:
- filtered: float32 [256, 24, 96, 128], P('band', 'sx', 'sy')
- gram: float32 [256, 256], P('band')
Inputs may be any that keep to these rules, and one draw needn't show every extreme that they name: `centers`: atom a's cell lies in the grid slab of the device numbered a // 4 along sx+sy, sy counting fastest; the first entry indexes the first grid dimension, the second the second.
All inputs are finite; a program needn't handle non-finite values.
Results may differ from a plain program's by a relative error of at most 0.0022.
Values may be sent and summed in bfloat16 or wider, within the bound.
A program may use at most 64 MiB of HBM per device.

v0:
```python
import jax
import jax.numpy as jnp
from jax import lax
from jax.sharding import PartitionSpec as P

stencil_weights = (
    -5369.0 / 1800.0,
    12.0 / 7.0,
    -15.0 / 56.0,
    10.0 / 189.0,
    -1.0 / 112.0,
    2.0 / 1925.0,
    -1.0 / 16632.0,
)
filter_center = 6.5
filter_half = 6.0
offsets_x = (0, -1, 1, 0, 0)
offsets_y = (0, 0, 0, -1, 1)


def from_behind(block, axis, distance):
    devices = range(lax.axis_size(axis))
    route = [(i - distance, i) for i in devices if i - distance in devices]
    return lax.ppermute(block, axis, route)


def extended(cells, sides, width):
    for axis, dim in sides:
        count = lax.axis_size(axis)
        ends = count - 1
        head = lax.slice_in_dim(cells, 0, width, axis=dim)
        tail = lax.slice_in_dim(cells, cells.shape[dim] - width, cells.shape[dim], axis=dim)
        cells = jnp.concatenate(
            [
                lax.ppermute(tail, axis, [(i, (i + 1) % count) for i in range(ends)]),
                cells,
                lax.ppermute(head, axis, [((i + 1) % count, i) for i in range(ends)]),
            ],
            axis=dim,
        )
    return cells


def second_sum(ext_x, ext_y, field):
    count_x = field.shape[1]
    count_y = field.shape[2]
    count_z = field.shape[3]
    padded_z = jnp.pad(field, ((0, 0), (0, 0), (0, 0), (6, 6)))
    total = 3.0 * stencil_weights[0] * field
    for step in range(1, 7):
        weight = stencil_weights[step]
        total = total + weight * (
            ext_x[:, 6 + step : 6 + step + count_x] + ext_x[:, 6 - step : 6 - step + count_x]
        )
        total = total + weight * (
            ext_y[:, :, 6 + step : 6 + step + count_y] + ext_y[:, :, 6 - step : 6 - step + count_y]
        )
        total = total + weight * (
            padded_z[:, :, :, 6 + step : 6 + step + count_z]
            + padded_z[:, :, :, 6 - step : 6 - step + count_z]
        )
    return total


def column_slots(centers, first_x, first_y, count_x, count_y):
    shift_x = jnp.array(offsets_x, jnp.int32)
    shift_y = jnp.array(offsets_y, jnp.int32)
    local_x = centers[:, 0:1] - first_x + shift_x[None, :]
    local_y = centers[:, 1:2] - first_y + shift_y[None, :]
    inner = count_x * count_y
    slots = jnp.where(
        local_x < 0,
        inner + local_y,
        jnp.where(
            local_x >= count_x,
            inner + count_y + local_y,
            jnp.where(
                local_y < 0,
                inner + 2 * count_y + local_x,
                jnp.where(
                    local_y >= count_y,
                    inner + 2 * count_y + count_x + local_x,
                    local_x * count_y + local_y,
                ),
            ),
        ),
    )
    return slots.reshape(-1)


def pass_x(strip, offset):
    return from_behind(strip.astype(jnp.bfloat16), "sx", offset).astype(strip.dtype)


def pass_y(strip, offset):
    return from_behind(strip, "sy", offset)


def nonlocal_term(field, ext_x, ext_y, slots, projectors, energies):
    batch, count_x, count_y, count_z = field.shape
    inner = count_x * count_y
    tiles = projectors.shape[2]
    atoms = projectors.shape[0]
    table = jnp.concatenate(
        [
            field.reshape(batch, inner, count_z),
            ext_x[:, 5],
            ext_x[:, 6 + count_x],
            ext_y[:, :, 5],
            ext_y[:, :, 6 + count_y],
        ],
        axis=1,
    )
    onehot = (slots[:, None] == jnp.arange(table.shape[1], dtype=jnp.int32)[None, :]).astype(
        jnp.float32
    )
    picked = jnp.einsum("kc,bcz->bkz", onehot, table, precision=lax.Precision.HIGHEST).reshape(
        batch, atoms, tiles, count_z
    )
    coeffs = jnp.einsum("aptz,batz->bap", projectors, picked, precision=lax.Precision.HIGHEST)
    weighted = coeffs * energies[None]
    spread = jnp.einsum(
        "aptz,bap->batz", projectors, weighted, precision=lax.Precision.HIGHEST
    ).reshape(batch, atoms * tiles, count_z)
    back = jnp.einsum("kc,bkz->bcz", onehot, spread, precision=lax.Precision.HIGHEST)
    result = back[:, :inner].reshape(batch, count_x, count_y, count_z)
    from_right = pass_x(back[:, inner : inner + count_y], -1)
    from_left = pass_x(back[:, inner + count_y : inner + 2 * count_y], 1)
    result = result.at[:, count_x - 1].add(from_right)
    result = result.at[:, 0].add(from_left)
    base_y = inner + 2 * count_y
    from_above = pass_y(back[:, base_y : base_y + count_x], -1)
    from_below = pass_y(back[:, base_y + count_x : base_y + 2 * count_x], 1)
    result = result.at[:, :, count_y - 1].add(from_above)
    result = result.at[:, :, 0].add(from_below)
    return result


def local(orbitals, potential, projectors, energies, centers):
    first_y = lax.axis_index("sy") * potential.shape[1]
    pot_all, proj_all, energy_all = (potential, projectors, energies)
    slots = column_slots(
        centers,
        lax.axis_index("sx") * potential.shape[0],
        first_y,
        orbitals.shape[1],
        orbitals.shape[2],
    )

    def apply_h(vector):
        ext_x = extended(vector, (("sx", 1),), 6)
        ext_y = extended(vector, (("sy", 2),), 6)
        kinetic = -0.5 * second_sum(ext_x, ext_y, vector)
        return (
            kinetic
            + pot_all[None] * vector
            + nonlocal_term(vector, ext_x, ext_y, slots, proj_all, energy_all)
        )

    previous = orbitals
    current = (apply_h(orbitals) - filter_center * orbitals) / filter_half
    following = 2.0 * (apply_h(current) - filter_center * current) / filter_half - previous
    previous, current = (current, following)
    rounded = current.astype(jnp.bfloat16)
    flat = rounded.reshape(rounded.shape[0], -1)
    partial_rows = lax.dot_general(
        flat,
        lax.all_gather(flat, "band", axis=0, tiled=True),
        (((1,), (1,)), ((), ())),
        preferred_element_type=jnp.float32,
    )
    cell_total = flat.shape[1] * lax.axis_size("sx") * lax.axis_size("sy")
    gram = lax.psum(partial_rows, ("sx", "sy")) / cell_total
    return (current, gram)


def solution(mesh):
    in_specs = (
        P("band", "sx", "sy", None),
        P("sx", "sy", None),
        P(("sx", "sy"), None, None, None),
        P(("sx", "sy"), None),
        P(("sx", "sy"), None),
    )
    out_specs = (P("band", "sx", "sy", None), P("band", None))
    return jax.shard_map(local, mesh=mesh, in_specs=in_specs, out_specs=out_specs, check_vma=False)
```

profile of v0, /device:TPU:128, one launch (start us, length us, event | category | flops | bytes accessed | tf_op | source)
XLA Modules:
  0.0 955.3 jit_solution(861587233101737842)
XLA Ops:
  8.6 4.6 collective-permute-start.1
  13.2 4.0 collective-permute-start.3
  18.5 3.1 copy.96
  21.8 15.3 %collective-permute-done = f32[64,6,6,128]{3,0,2,1:T(8,128)S(1)} collective-permute-done((f32[64,6,6,128]{3,0,2,1:T(8,128)}, f32[64,6,6,128]{3,0,2,1:T(8,128)S(1)}, u32[]{:S(2)}, u32[]{:S(2)}) %collective-permute-start) | collective-permute-done | bytes 1179680 | tf_op jit(solution)/shard_map/ppermute | solution.py:37
  41.1 2.0 copy_dynamic-update-slice_fusion.2
  43.1 2.5 copy_dynamic-update-slice_fusion
  45.6 25.1 %collective-permute-done.2 = f32[64,6,6,128]{3,0,2,1:T(8,128)} collective-permute-done((f32[64,6,6,128]{3,0,2,1:T(8,128)}, f32[64,6,6,128]{3,0,2,1:T(8,128)}, u32[]{:S(2)}, u32[]{:S(2)}) %collective-permute-start.2) | collective-permute-done | bytes 1179680 | tf_op jit(solution)/shard_map/ppermute | solution.py:37
  70.7 3.1 copy_dynamic-update-slice_fusion.3
  74.7 14.2 %concatenate.86 = f32[64,60,128]{2,1,0:T(8,128)} concatenate(f32[64,36,128]{2,1,0:T(8,128)} %copy.96, f32[64,6,128]{2,1,0:T(8,128)} %bitcast.115, f32[64,6,128]{2,1,0:T(8,128)S(1)} %bitcast.114, f32[64,6,128]{2,1,0:T(8,128)} %get-tuple-element.126, f32[64,6,128]{2,1,0:T(8,128)} %get-tuple-element.125), dimensions={1} | concatenate | bytes 3932160 | tf_op jit(solution)/shard_map/concatenate | solution.py:104
  88.9 2.5 convolution_bitcast_fusion.3
  98.2 4.7 collective-permute-start.5
  104.2 5.3 collective-permute-start.7
  109.4 1.9 copy.78
  111.4 1.8 copy.79
  113.2 1.8 copy.102
  115.3 6.1 scatter-add.29
  124.9 34.7 %broadcast_multiply_fusion = (f32[64,6,6,128]{3,1,0,2:T(8,128)S(1)}, f32[64,6,6,128]{3,1,0,2:T(8,128)}) fusion(f32[64,6,6,128]{3,1,0,2:T(8,128)} %get-tuple-element.116, f32[64,6,6,128]{3,1,0,2:T(8,128)} %fusion.135, f32[6,6,128]{2,0,1:T(8,128)S(1)} %copy.90, f32[64,6,6,128]{3,0,2,1:T(8,128)} %collective-permute-done.3, ...), kind=kLoop, calls=%fused_computation.225 | loop fusion | flops 21233664 | bytes 21252096 | tf_op jit(solution)/shard_map/div | solution.py:161
  162.5 4.6 collective-permute-start.11
  167.1 4.8 collective-permute-start.9
  172.7 15.8 %collective-permute-done.8 = f32[64,6,6,128]{3,0,2,1:T(8,128)S(1)} collective-permute-done((f32[64,6,6,128]{3,0,2,1:T(8,128)S(1)}, f32[64,6,6,128]{3,0,2,1:T(8,128)S(1)}, u32[]{:S(2)}, u32[]{:S(2)}) %collective-permute-start.8) | collective-permute-done | bytes 1179680 | tf_op jit(solution)/shard_map/ppermute | solution.py:37
  189.6 2.6 collective-permute-done.10
  196.3 6.5 concatenate.91
  210.5 5.3 collective-permute-start.13
  217.2 4.8 collective-permute-start.15
  222.0 1.9 copy.105
  223.9 1.9 copy.107
  225.9 1.8 copy.128
  227.9 6.2 scatter-add.35
  237.5 15.2 %fusion.152 = (bf16[64,6,6,128]{3,1,0,2:T(8,128)(2,1)S(1)}, f32[64,6,6,128]{3,1,0,2:T(8,128)}) fusion(f32[64,6,6,128]{3,0,2,1:T(8,128)S(1)} %copy-done.4, f32[64,6,6,128]{3,1,0,2:T(8,128)} %get-tuple-element.107, f32[64,6,6,128]{3,1,0,2:T(8,128)} %fusion.133, f32[6,6,128]{2,0,1:T(8,128)S(1)} %copy.116, f32[64,6,6,128]{3,1,0,2:T(8,128)} %copy-done.5, ...), kind=kLoop, calls=%fused_computation.274 | loop fusion | flops 24772608 | bytes 11225088 | tf_op jit(solution)/shard_map/convert_element_type | solution.py:164
  255.0 65.0 %all-gather.2.cloned.1.call-done = bf16[256,4608]{1,0:T(8,128)(2,1)} async-done(((bf16[64,4608]{1,0:T(8,128)(2,1)}), bf16[256,4608]{1,0:T(8,128)(2,1)}) %all-gather.2.cloned.1.call-update) | async-done | bytes 2359312 | tf_op jit(solution)/shard_map/all_gather | solution.py:168
  320.0 3.3 fusion.160
  324.6 622.4 %all-reduce.4.cloned.1.call-done = f32[64,256]{1,0:T(8,128)} async-done(((f32[64,256]{1,0:T(8,128)}), f32[64,256]{1,0:T(8,128)}) %all-reduce.4.cloned.1.call-update) | async-done | bytes 65552 | tf_op jit(solution)/shard_map/psum | solution.py:173
  (122 shorter events, 45.8 us)
Async XLA Ops:
  7.2 84.3 %copy-start = (f32[4,4,5,128]{3,1,2,0:T(4,128)S(1)}, f32[4,4,5,128]{3,1,2,0:T(4,128)}, u32[]{:S(2)}) copy-start(f32[4,4,5,128]{3,1,2,0:T(4,128)} %param.25) | copy-start | bytes 122884
  7.2 14.5 %copy-start.19 = (s32[5]{0:T(128)S(1)}, s32[5]{0:T(128)}, u32[]{:S(2)}) copy-start(s32[5]{0:T(128)} %constant.246.clone) | copy-start | bytes 64
  7.2 14.5 %copy-start.20 = (s32[5]{0:T(128)S(1)}, s32[5]{0:T(128)}, u32[]{:S(2)}) copy-start(s32[5]{0:T(128)} %constant.247.clone) | copy-start | bytes 64
  7.2 14.4 %copy-start.18 = (s32[4,2]{0,1:T(2,128)S(1)}, s32[4,2]{0,1:T(2,128)}, u32[]{:S(2)}) copy-start(s32[4,2]{0,1:T(2,128)} %param.27) | copy-start | bytes 100
  7.2 14.6 %copy-start.16 = (f32[6,6,128]{2,1,0:T(8,128)S(1)}, f32[6,6,128]{2,1,0:T(8,128)}, u32[]{:S(2)}) copy-start(f32[6,6,128]{2,1,0:T(8,128)} %param.24) | copy-start | bytes 55300
  7.2 312.8 %all-gather.2.cloned.1.call-start = ((), (), s32[]{:S(2)}) async-start(), calls=%async_computation | async-start | bytes 2949120 | tf_op jit(solution)/shard_map/all_gather | solution.py:168
  7.3 29.8 %collective-permute-start = (f32[64,6,6,128]{3,0,2,1:T(8,128)}, f32[64,6,6,128]{3,0,2,1:T(8,128)S(1)}, u32[]{:S(2)}, u32[]{:S(2)}) collective-permute-start(f32[64,6,6,128]{3,0,2,1:T(8,128)} %param.23), channel_id=1, source_target_pairs={{16,0},{32,16},{48,32},{17,1},{33,17},{49,33},{18,2},{34,18},{50,3... | collective-permute-start | bytes 3538952 | tf_op jit(solution)/shard_map/ppermute | solution.py:37
  8.6 29.8 %collective-permute-start.1 = (f32[64,6,6,128]{3,0,2,1:T(8,128)}, f32[64,6,6,128]{3,0,2,1:T(8,128)S(1)}, u32[]{:S(2)}, u32[]{:S(2)}) collective-permute-start(f32[64,6,6,128]{3,0,2,1:T(8,128)} %param.23), channel_id=1, source_target_pairs={{0,16},{16,32},{32,48},{1,17},{17,33},{33,49},{2,18},{18,34},{34,5... | collective-permute-start | bytes 3538952 | tf_op jit(solution)/shard_map/ppermute | solution.py:35
  13.2 27.9 %collective-permute-start.3 = (f32[64,6,6,128]{3,0,2,1:T(8,128)}, f32[64,6,6,128]{3,0,2,1:T(8,128)}, u32[]{:S(2)}, u32[]{:S(2)}) collective-permute-start(f32[64,6,6,128]{3,0,2,1:T(8,128)} %param.23), channel_id=1, source_target_pairs={{0,1},{1,2},{2,3},{3,4},{4,5},{5,6},{6,7},{7,8},{8,9},{9,10},{10,1... | collective-permute-start | bytes 3538952 | tf_op jit(solution)/shard_map/ppermute | solution.py:35
  17.2 53.5 %collective-permute-start.2 = (f32[64,6,6,128]{3,0,2,1:T(8,128)}, f32[64,6,6,128]{3,0,2,1:T(8,128)}, u32[]{:S(2)}, u32[]{:S(2)}) collective-permute-start(f32[64,6,6,128]{3,0,2,1:T(8,128)} %param.23), channel_id=1, source_target_pairs={{1,0},{2,1},{3,2},{4,3},{5,4},{6,5},{7,6},{8,7},{9,8},{10,9},{11,1... | collective-permute-start | bytes 3538952 | tf_op jit(solution)/shard_map/ppermute | solution.py:37
  39.5 3.6 copy-start.3
  95.7 17.5 %collective-permute-start.4 = (bf16[64,6,128]{2,0,1:T(8,128)(2,1)S(1)}, bf16[64,6,128]{2,0,1:T(8,128)(2,1)S(1)}, u32[]{:S(2)}, u32[]{:S(2)}) collective-permute-start(bf16[64,6,128]{2,0,1:T(8,128)(2,1)S(1)} %get-tuple-element.122), channel_id=1, source_target_pairs={{16,0},{32,16},{48,32},{17,1},{33,17},{49,33},{18,2},{34,18},{50,3... | collective-permute-start | bytes 294920 | tf_op jit(solution)/shard_map/ppermute | solution.py:24
  97.9 11.5 %copy-start.9 = (f32[64,6,6,128]{3,0,2,1:T(8,128)S(1)}, f32[64,6,6,128]{3,0,2,1:T(8,128)}, u32[]{:S(2)}) copy-start(f32[64,6,6,128]{3,0,2,1:T(8,128)} %copy-done.8) | copy-start | bytes 3538948
  98.2 13.2 %copy-start.11 = (f32[64,6,6,128]{3,0,2,1:T(8,128)S(1)}, f32[64,6,6,128]{3,0,2,1:T(8,128)}, u32[]{:S(2)}) copy-start(f32[64,6,6,128]{3,0,2,1:T(8,128)} %copy-done.10) | copy-start | bytes 3538948
  98.2 16.9 %collective-permute-start.5 = (bf16[64,6,128]{2,0,1:T(8,128)(2,1)S(1)}, bf16[64,6,128]{2,0,1:T(8,128)(2,1)S(1)}, u32[]{:S(2)}, u32[]{:S(2)}) collective-permute-start(bf16[64,6,128]{2,0,1:T(8,128)(2,1)S(1)} %get-tuple-element.121), channel_id=1, source_target_pairs={{0,16},{16,32},{32,48},{1,17},{17,33},{33,49},{2,18},{18,34},{34,5... | collective-permute-start | bytes 294920 | tf_op jit(solution)/shard_map/ppermute | solution.py:24
  102.9 18.5 %collective-permute-start.6 = (f32[64,6,128]{2,1,0:T(8,128)}, f32[64,6,128]{2,1,0:T(8,128)}, u32[]{:S(2)}, u32[]{:S(2)}) collective-permute-start(f32[64,6,128]{2,1,0:T(8,128)} %get-tuple-element.111), channel_id=1, source_target_pairs={{1,0},{2,1},{3,2},{4,3},{5,4},{6,5},{7,6},{8,7},{9,8},{10,9},{11,1... | collective-permute-start | bytes 589832 | tf_op jit(solution)/shard_map/ppermute | solution.py:24
  104.2 19.0 %collective-permute-start.7 = (f32[64,6,128]{2,1,0:T(8,128)}, f32[64,6,128]{2,1,0:T(8,128)}, u32[]{:S(2)}, u32[]{:S(2)}) collective-permute-start(f32[64,6,128]{2,1,0:T(8,128)} %get-tuple-element.110), channel_id=1, source_target_pairs={{0,1},{1,2},{2,3},{3,4},{4,5},{5,6},{6,7},{7,8},{8,9},{9,10},{10,1... | collective-permute-start | bytes 589832 | tf_op jit(solution)/shard_map/ppermute | solution.py:24
  159.6 13.1 %copy-start.1 = (f32[64,6,6,128]{3,1,0,2:T(8,128)}, f32[64,6,6,128]{3,1,0,2:T(8,128)S(1)}, u32[]{:S(2)}) copy-start(f32[64,6,6,128]{3,1,0,2:T(8,128)S(1)} %get-tuple-element.106) | copy-start | bytes 3538948
  159.9 28.7 %collective-permute-start.8 = (f32[64,6,6,128]{3,0,2,1:T(8,128)S(1)}, f32[64,6,6,128]{3,0,2,1:T(8,128)S(1)}, u32[]{:S(2)}, u32[]{:S(2)}) collective-permute-start(f32[64,6,6,128]{3,0,2,1:T(8,128)S(1)} %copy.104), channel_id=1, source_target_pairs={{16,0},{32,16},{48,32},{17,1},{33,17},{49,33},{18,2},{34,18},{50,3... | collective-permute-start | bytes 3538952 | tf_op jit(solution)/shard_map/ppermute | solution.py:37
  161.2 31.0 %collective-permute-start.10 = (f32[64,6,6,128]{3,0,2,1:T(8,128)S(1)}, f32[64,6,6,128]{3,0,2,1:T(8,128)S(1)}, u32[]{:S(2)}, u32[]{:S(2)}) collective-permute-start(f32[64,6,6,128]{3,0,2,1:T(8,128)S(1)} %copy.104), channel_id=1, source_target_pairs={{1,0},{2,1},{3,2},{4,3},{5,4},{6,5},{7,6},{8,7},{9,8},{10,9},{11,1... | collective-permute-start | bytes 3538952 | tf_op jit(solution)/shard_map/ppermute | solution.py:37
  162.5 30.4 %collective-permute-start.11 = (f32[64,6,6,128]{3,0,2,1:T(8,128)S(1)}, f32[64,6,6,128]{3,0,2,1:T(8,128)S(1)}, u32[]{:S(2)}, u32[]{:S(2)}) collective-permute-start(f32[64,6,6,128]{3,0,2,1:T(8,128)S(1)} %copy.104), channel_id=1, source_target_pairs={{0,1},{1,2},{2,3},{3,4},{4,5},{5,6},{6,7},{7,8},{8,9},{9,10},{10,1... | collective-permute-start | bytes 3538952 | tf_op jit(solution)/shard_map/ppermute | solution.py:35
  167.1 28.0 %collective-permute-start.9 = (f32[64,6,6,128]{3,0,2,1:T(8,128)S(1)}, f32[64,6,6,128]{3,0,2,1:T(8,128)S(1)}, u32[]{:S(2)}, u32[]{:S(2)}) collective-permute-start(f32[64,6,6,128]{3,0,2,1:T(8,128)S(1)} %copy.104), channel_id=1, source_target_pairs={{0,16},{16,32},{32,48},{1,17},{17,33},{33,49},{2,18},{18,34},{34,5... | collective-permute-start | bytes 3538952 | tf_op jit(solution)/shard_map/ppermute | solution.py:35
  208.0 17.8 %collective-permute-start.12 = (bf16[64,6,128]{2,0,1:T(8,128)(2,1)S(1)}, bf16[64,6,128]{2,0,1:T(8,128)(2,1)S(1)}, u32[]{:S(2)}, u32[]{:S(2)}) collective-permute-start(bf16[64,6,128]{2,0,1:T(8,128)(2,1)S(1)} %get-tuple-element.120), channel_id=1, source_target_pairs={{16,0},{32,16},{48,32},{17,1},{33,17},{49,33},{18,2},{34,18},{50,3... | collective-permute-start | bytes 294920 | tf_op jit(solution)/shard_map/ppermute | solution.py:24
  210.3 11.7 %copy-start.13 = (f32[64,6,6,128]{3,0,2,1:T(8,128)S(1)}, f32[64,6,6,128]{3,0,2,1:T(8,128)}, u32[]{:S(2)}) copy-start(f32[64,6,6,128]{3,0,2,1:T(8,128)} %copy-done.12) | copy-start | bytes 3538948
  210.5 13.4 %copy-start.15 = (f32[64,6,6,128]{3,0,2,1:T(8,128)S(1)}, f32[64,6,6,128]{3,0,2,1:T(8,128)}, u32[]{:S(2)}) copy-start(f32[64,6,6,128]{3,0,2,1:T(8,128)} %copy-done.14) | copy-start | bytes 3538948
  210.5 17.2 %collective-permute-start.13 = (bf16[64,6,128]{2,0,1:T(8,128)(2,1)S(1)}, bf16[64,6,128]{2,0,1:T(8,128)(2,1)S(1)}, u32[]{:S(2)}, u32[]{:S(2)}) collective-permute-start(bf16[64,6,128]{2,0,1:T(8,128)(2,1)S(1)} %get-tuple-element.119), channel_id=1, source_target_pairs={{0,16},{16,32},{32,48},{1,17},{17,33},{33,49},{2,18},{18,34},{34,5... | collective-permute-start | bytes 294920 | tf_op jit(solution)/shard_map/ppermute | solution.py:24
  215.9 18.3 %collective-permute-start.14 = (f32[64,6,128]{2,1,0:T(8,128)}, f32[64,6,128]{2,1,0:T(8,128)S(1)}, u32[]{:S(2)}, u32[]{:S(2)}) collective-permute-start(f32[64,6,128]{2,1,0:T(8,128)} %get-tuple-element.109), channel_id=1, source_target_pairs={{1,0},{2,1},{3,2},{4,3},{5,4},{6,5},{7,6},{8,7},{9,8},{10,9},{11,1... | collective-permute-start | bytes 589832 | tf_op jit(solution)/shard_map/ppermute | solution.py:24
  217.2 18.7 %collective-permute-start.15 = (f32[64,6,128]{2,1,0:T(8,128)}, f32[64,6,128]{2,1,0:T(8,128)S(1)}, u32[]{:S(2)}, u32[]{:S(2)}) collective-permute-start(f32[64,6,128]{2,1,0:T(8,128)} %get-tuple-element.108), channel_id=1, source_target_pairs={{0,1},{1,2},{2,3},{3,4},{4,5},{5,6},{6,7},{7,8},{8,9},{9,10},{10,1... | collective-permute-start | bytes 589832 | tf_op jit(solution)/shard_map/ppermute | solution.py:24
  227.7 9.8 %copy-start.2 = (f32[64,6,6,128]{3,1,0,2:T(8,128)S(1)}, f32[64,6,6,128]{3,1,0,2:T(8,128)}, u32[]{:S(2)}) copy-start(f32[64,6,6,128]{3,1,0,2:T(8,128)} %copy-done.1) | copy-start | bytes 3538948
  227.7 9.8 %copy-start.4 = (f32[64,6,6,128]{3,0,2,1:T(8,128)S(1)}, f32[64,6,6,128]{3,0,2,1:T(8,128)}, u32[]{:S(2)}) copy-start(f32[64,6,6,128]{3,0,2,1:T(8,128)} %param.23) | copy-start | bytes 3538948
  254.9 68.4 %copy-start.7 = (f32[64,6,6,128]{3,1,0,2:T(8,128)S(1)}, f32[64,6,6,128]{3,1,0,2:T(8,128)}, u32[]{:S(2)}) copy-start(f32[64,6,6,128]{3,1,0,2:T(8,128)} %get-tuple-element.105) | copy-start | bytes 3538948
  254.9 692.0 %all-reduce.4.cloned.1.call-start = ((), (), s32[]{:S(2)}) async-start(), calls=%async_computation.1 | async-start | bytes 131072 | tf_op jit(solution)/shard_map/psum | solution.py:173
  (7 other events, 12.4 us)
Sparse Core Ops, SparseCore 0:
  255.0 64.9 all-gather.1
  323.5 623.4 all-reduce.3
where the time goes:
time: 957 us; the launch traced here: 955 us
  waiting for transfers between devices  749 us (78%)
  local copies, waits for them, and re-layouts  71.6 us (7%)
  other arithmetic  58.9 us (6%)
  starting transfers between devices  48.6 us (5%)
  between operations  14.6 us (2%)
  matrix products  12.6 us (1%)
    psum x1, waiting for transfers between devices, local(): gram = lax.psum(partial_rows, ('sx', 'sy')) / cell_total  622 us
    all_gather x1, waiting for transfers between devices, local(): lax.all_gather(flat, 'band', axis=0, tiled=True)  65 us
    ppermute x4, waiting for transfers between devices, extended(): lax.ppermute(head, axis, [((i + 1) % count, i) for i in range(ends)])  58.8 us
    div x1, other arithmetic, local(): current = (apply_h(orbitals) - filter_center * orbitals) / filter_half  34.7 us
    ppermute x8, starting transfers between devices, from_behind(): return lax.ppermute(block, axis, route)  25.2 us
    concatenate x2, local copies, waits for them, and re-layouts, nonlocal_term(): jnp.concatenate([field.reshape(batch, inner, count_z), ext_x[:, 5], ext_x...  20.6 us
  transfers between devices with their start and end apart: 18, of which 8 were waited for; matrix products, arithmetic and copies ran while one was open for 5% of the time, Pallas kernels for 0%

commit v1 on v0

--- a/solution.py
+++ b/solution.py
@@ -170,7 +170,7 @@
         preferred_element_type=jnp.float32,
     )
     cell_total = flat.shape[1] * lax.axis_size("sx") * lax.axis_size("sy")
-    gram = lax.psum(partial_rows, ("sx", "sy")) / cell_total
+    gram = lax.psum(lax.psum(partial_rows, "sx"), "sy") / cell_total
     return (current, gram)
 
 

time: 957 us -> 535 us (0.56)
  waiting for transfers between devices: 749 us -> 325 us
    psum x1 -> x2, waiting for transfers between devices: 622 us -> 198 us  [local(): gram = lax.psum(lax.psum(partial_rows, 'sx'), 'sy') / cell_total]
  transfers between devices with their start and end apart: 18 -> 19, of which waited for: 8 -> 9; matrix products, arithmetic and copies ran while one was open for 5% -> 8% of each run, Pallas kernels for 0% -> 0%
where the time goes in v1:
time: 535 us; the launch traced here: 531 us
  waiting for transfers between devices  325 us (61%)
  local copies, waits for them, and re-layouts  71.6 us (13%)
  other arithmetic  58.9 us (11%)
  starting transfers between devices  48.6 us (9%)
  between operations  14.3 us (3%)
  matrix products  12.6 us (2%)
    psum x2, waiting for transfers between devices, local(): gram = lax.psum(lax.psum(partial_rows, 'sx'), 'sy') / cell_total  198 us
    all_gather x1, waiting for transfers between devices, local(): lax.all_gather(flat, 'band', axis=0, tiled=True)  65 us
    ppermute x4, waiting for transfers between devices, extended(): lax.ppermute(head, axis, [((i + 1) % count, i) for i in range(ends)])  58.8 us
    div x1, other arithmetic, local(): current = (apply_h(orbitals) - filter_center * orbitals) / filter_half  34.7 us
    ppermute x8, starting transfers between devices, from_behind(): return lax.ppermute(block, axis, route)  25.2 us
    concatenate x2, local copies, waits for them, and re-layouts, nonlocal_term(): jnp.concatenate([field.reshape(batch, inner, count_z), ext_x[:, 5], ext_x...  20.6 us
    ppermute x4, starting transfers between devices, extended(): lax.ppermute(tail, axis, [(i, (i + 1) % count) for i in range(ends)])  18.1 us
    convert_element_type x1, other arithmetic, local(): rounded = current.astype(jnp.bfloat16)  15.2 us
  transfers between devices with their start and end apart: 19, of which 9 were waited for; matrix products, arithmetic and copies ran while one was open for 8% of the time, Pallas kernels for 0%

profile of v1, /device:TPU:128, one launch (start us, length us, event | category | flops | bytes accessed | tf_op | source)
XLA Modules:
  0.0 530.9 jit_solution(10505787169882320534)
XLA Ops:
  8.6 4.6 collective-permute-start.1
  13.2 4.0 collective-permute-start.3
  18.5 3.1 copy.96
  21.8 15.3 %collective-permute-done = f32[64,6,6,128]{3,0,2,1:T(8,128)S(1)} collective-permute-done((f32[64,6,6,128]{3,0,2,1:T(8,128)}, f32[64,6,6,128]{3,0,2,1:T(8,128)S(1)}, u32[]{:S(2)}, u32[]{:S(2)}) %collective-permute-start) | collective-permute-done | bytes 1179680 | tf_op jit(solution)/shard_map/ppermute | solution.py:37
  41.1 2.0 copy_dynamic-update-slice_fusion.2
  43.1 2.5 copy_dynamic-update-slice_fusion
  45.6 25.1 %collective-permute-done.2 = f32[64,6,6,128]{3,0,2,1:T(8,128)} collective-permute-done((f32[64,6,6,128]{3,0,2,1:T(8,128)}, f32[64,6,6,128]{3,0,2,1:T(8,128)}, u32[]{:S(2)}, u32[]{:S(2)}) %collective-permute-start.2) | collective-permute-done | bytes 1179680 | tf_op jit(solution)/shard_map/ppermute | solution.py:37
  70.7 3.1 copy_dynamic-update-slice_fusion.3
  74.7 14.2 %concatenate.86 = f32[64,60,128]{2,1,0:T(8,128)} concatenate(f32[64,36,128]{2,1,0:T(8,128)} %copy.96, f32[64,6,128]{2,1,0:T(8,128)} %bitcast.115, f32[64,6,128]{2,1,0:T(8,128)S(1)} %bitcast.114, f32[64,6,128]{2,1,0:T(8,128)} %get-tuple-element.126, f32[64,6,128]{2,1,0:T(8,128)} %get-tuple-element.125), dimensions={1} | concatenate | bytes 3932160 | tf_op jit(solution)/shard_map/concatenate | solution.py:104
  88.9 2.5 convolution_bitcast_fusion.3
  98.2 4.7 collective-permute-start.5
  104.2 5.3 collective-permute-start.7
  109.4 1.9 copy.78
  111.4 1.8 copy.79
  115.3 6.1 %scatter-add.29 = f32[64,6,6,128]{3,1,0,2:T(8,128)} dynamic-update-slice(f32[64,6,6,128]{3,1,0,2:T(8,128)} %copy.102, f32[64,1,6,128]{3,1,0,2:T(1,128)S(1)} %add.432, s32[]{:T(128)} %constant.233.clone.1, s32[]{:T(128)} %constant.233.clone.1, s32[]{:T(128)} %constant.233.clone.1, s32[]{:T(128)} %constant.233.clone.1) | dynamic-update-slice | bytes 393220 | tf_op jit(solution)/shard_map/scatter-add | solution.py:130
  124.9 34.7 %broadcast_multiply_fusion = (f32[64,6,6,128]{3,1,0,2:T(8,128)S(1)}, f32[64,6,6,128]{3,1,0,2:T(8,128)}) fusion(f32[64,6,6,128]{3,1,0,2:T(8,128)} %get-tuple-element.116, f32[64,6,6,128]{3,1,0,2:T(8,128)} %fusion.135, f32[6,6,128]{2,0,1:T(8,128)S(1)} %copy.90, f32[64,6,6,128]{3,0,2,1:T(8,128)} %collective-permute-done.3, ...), kind=kLoop, calls=%fused_computation.225 | loop fusion | flops 21233664 | bytes 21252096 | tf_op jit(solution)/shard_map/div | solution.py:161
  162.5 4.6 collective-permute-start.11
  167.1 4.8 collective-permute-start.9
  172.7 15.8 %collective-permute-done.8 = f32[64,6,6,128]{3,0,2,1:T(8,128)S(1)} collective-permute-done((f32[64,6,6,128]{3,0,2,1:T(8,128)S(1)}, f32[64,6,6,128]{3,0,2,1:T(8,128)S(1)}, u32[]{:S(2)}, u32[]{:S(2)}) %collective-permute-start.8) | collective-permute-done | bytes 1179680 | tf_op jit(solution)/shard_map/ppermute | solution.py:37
  189.6 2.6 collective-permute-done.10
  196.3 6.5 %concatenate.91 = f32[64,60,128]{2,1,0:T(8,128)S(1)} concatenate(f32[64,36,128]{2,1,0:T(8,128)S(1)} %copy.122, f32[64,6,128]{2,1,0:T(8,128)} %bitcast.117, f32[64,6,128]{2,1,0:T(8,128)} %bitcast.116, f32[64,6,128]{2,1,0:T(8,128)} %slice_bitcast_fusion.1, f32[64,6,128]{2,1,0:T(8,128)} %slice_bitcast_fusion), dimensions={1} | concatenate | bytes 3932160 | tf_op jit(solution)/shard_map/concatenate | solution.py:104
  210.5 5.3 %collective-permute-start.13 = (bf16[64,6,128]{2,0,1:T(8,128)(2,1)S(1)}, bf16[64,6,128]{2,0,1:T(8,128)(2,1)S(1)}, u32[]{:S(2)}, u32[]{:S(2)}) collective-permute-start(bf16[64,6,128]{2,0,1:T(8,128)(2,1)S(1)} %get-tuple-element.119), channel_id=1, source_target_pairs={{0,16},{16,32},{32,48},{1,17},{17,33},{33,49},{2,18},{18,34},{34,5... | collective-permute-start | bytes 294920 | tf_op jit(solution)/shard_map/ppermute | solution.py:24
  217.2 4.8 collective-permute-start.15
  222.0 1.9 copy.105
  223.9 1.9 copy.107
  225.9 1.8 copy.128
  227.9 6.2 %scatter-add.35 = f32[64,6,6,128]{3,1,0,2:T(8,128)} dynamic-update-slice(f32[64,6,6,128]{3,1,0,2:T(8,128)} %copy.128, f32[64,1,6,128]{3,1,0,2:T(1,128)S(1)} %add.474, s32[]{:T(128)} %constant.233.clone.1, s32[]{:T(128)} %constant.233.clone.1, s32[]{:T(128)} %constant.233.clone.1, s32[]{:T(128)} %constant.233.clone.1) | dynamic-update-slice | bytes 393220 | tf_op jit(solution)/shard_map/scatter-add | solution.py:130
  237.5 15.2 %fusion.152 = (bf16[64,6,6,128]{3,1,0,2:T(8,128)(2,1)S(1)}, f32[64,6,6,128]{3,1,0,2:T(8,128)}) fusion(f32[64,6,6,128]{3,0,2,1:T(8,128)S(1)} %copy-done.4, f32[64,6,6,128]{3,1,0,2:T(8,128)} %get-tuple-element.107, f32[64,6,6,128]{3,1,0,2:T(8,128)} %fusion.133, f32[6,6,128]{2,0,1:T(8,128)S(1)} %copy.116, f32[64,6,6,128]{3,1,0,2:T(8,128)} %copy-done.5, ...), kind=kLoop, calls=%fused_computation.274 | loop fusion | flops 24772608 | bytes 11225088 | tf_op jit(solution)/shard_map/convert_element_type | solution.py:164
  255.0 65.0 %all-gather.2.cloned.1.call-done = bf16[256,4608]{1,0:T(8,128)(2,1)} async-done(((bf16[64,4608]{1,0:T(8,128)(2,1)}), bf16[256,4608]{1,0:T(8,128)(2,1)}) %all-gather.2.cloned.1.call-update) | async-done | bytes 2359312 | tf_op jit(solution)/shard_map/all_gather | solution.py:168
  320.0 3.3 fusion.160
  323.4 49.8 %all-reduce.5.cloned.1.call-done = f32[64,256]{1,0:T(8,128)} async-done(((f32[64,256]{1,0:T(8,128)}), f32[64,256]{1,0:T(8,128)}) %all-reduce.5.cloned.1.call-update) | async-done | bytes 65552 | tf_op jit(solution)/shard_map/psum | solution.py:173
  374.5 148.5 %all-reduce.7.cloned.1.call-done = f32[64,256]{1,0:T(8,128)} async-done(((f32[64,256]{1,0:T(8,128)}), f32[64,256]{1,0:T(8,128)}) %all-reduce.7.cloned.1.call-update) | async-done | bytes 65552 | tf_op jit(solution)/shard_map/psum | solution.py:173
  (125 shorter events, 47.7 us)
Async XLA Ops:
  7.2 84.3 %copy-start = (f32[4,4,5,128]{3,1,2,0:T(4,128)S(1)}, f32[4,4,5,128]{3,1,2,0:T(4,128)}, u32[]{:S(2)}) copy-start(f32[4,4,5,128]{3,1,2,0:T(4,128)} %param.25) | copy-start | bytes 122884
  7.2 14.5 %copy-start.19 = (s32[5]{0:T(128)S(1)}, s32[5]{0:T(128)}, u32[]{:S(2)}) copy-start(s32[5]{0:T(128)} %constant.246.clone) | copy-start | bytes 64
  7.2 14.5 %copy-start.20 = (s32[5]{0:T(128)S(1)}, s32[5]{0:T(128)}, u32[]{:S(2)}) copy-start(s32[5]{0:T(128)} %constant.247.clone) | copy-start | bytes 64
  7.2 14.4 %copy-start.18 = (s32[4,2]{0,1:T(2,128)S(1)}, s32[4,2]{0,1:T(2,128)}, u32[]{:S(2)}) copy-start(s32[4,2]{0,1:T(2,128)} %param.27) | copy-start | bytes 100
  7.2 14.6 %copy-start.16 = (f32[6,6,128]{2,1,0:T(8,128)S(1)}, f32[6,6,128]{2,1,0:T(8,128)}, u32[]{:S(2)}) copy-start(f32[6,6,128]{2,1,0:T(8,128)} %param.24) | copy-start | bytes 55300
  7.2 312.8 %all-gather.2.cloned.1.call-start = ((), (), s32[]{:S(2)}) async-start(), calls=%async_computation | async-start | bytes 2949120 | tf_op jit(solution)/shard_map/all_gather | solution.py:168
  7.3 29.8 %collective-permute-start = (f32[64,6,6,128]{3,0,2,1:T(8,128)}, f32[64,6,6,128]{3,0,2,1:T(8,128)S(1)}, u32[]{:S(2)}, u32[]{:S(2)}) collective-permute-start(f32[64,6,6,128]{3,0,2,1:T(8,128)} %param.23), channel_id=1, source_target_pairs={{16,0},{32,16},{48,32},{17,1},{33,17},{49,33},{18,2},{34,18},{50,3... | collective-permute-start | bytes 3538952 | tf_op jit(solution)/shard_map/ppermute | solution.py:37
  8.6 29.8 %collective-permute-start.1 = (f32[64,6,6,128]{3,0,2,1:T(8,128)}, f32[64,6,6,128]{3,0,2,1:T(8,128)S(1)}, u32[]{:S(2)}, u32[]{:S(2)}) collective-permute-start(f32[64,6,6,128]{3,0,2,1:T(8,128)} %param.23), channel_id=1, source_target_pairs={{0,16},{16,32},{32,48},{1,17},{17,33},{33,49},{2,18},{18,34},{34,5... | collective-permute-start | bytes 3538952 | tf_op jit(solution)/shard_map/ppermute | solution.py:35
  13.2 27.9 %collective-permute-start.3 = (f32[64,6,6,128]{3,0,2,1:T(8,128)}, f32[64,6,6,128]{3,0,2,1:T(8,128)}, u32[]{:S(2)}, u32[]{:S(2)}) collective-permute-start(f32[64,6,6,128]{3,0,2,1:T(8,128)} %param.23), channel_id=1, source_target_pairs={{0,1},{1,2},{2,3},{3,4},{4,5},{5,6},{6,7},{7,8},{8,9},{9,10},{10,1... | collective-permute-start | bytes 3538952 | tf_op jit(solution)/shard_map/ppermute | solution.py:35
  17.2 53.5 %collective-permute-start.2 = (f32[64,6,6,128]{3,0,2,1:T(8,128)}, f32[64,6,6,128]{3,0,2,1:T(8,128)}, u32[]{:S(2)}, u32[]{:S(2)}) collective-permute-start(f32[64,6,6,128]{3,0,2,1:T(8,128)} %param.23), channel_id=1, source_target_pairs={{1,0},{2,1},{3,2},{4,3},{5,4},{6,5},{7,6},{8,7},{9,8},{10,9},{11,1... | collective-permute-start | bytes 3538952 | tf_op jit(solution)/shard_map/ppermute | solution.py:37
  95.7 17.5 %collective-permute-start.4 = (bf16[64,6,128]{2,0,1:T(8,128)(2,1)S(1)}, bf16[64,6,128]{2,0,1:T(8,128)(2,1)S(1)}, u32[]{:S(2)}, u32[]{:S(2)}) collective-permute-start(bf16[64,6,128]{2,0,1:T(8,128)(2,1)S(1)} %get-tuple-element.122), channel_id=1, source_target_pairs={{16,0},{32,16},{48,32},{17,1},{33,17},{49,33},{18,2},{34,18},{50,3... | collective-permute-start | bytes 294920 | tf_op jit(solution)/shard_map/ppermute | solution.py:24
  97.9 11.5 %copy-start.9 = (f32[64,6,6,128]{3,0,2,1:T(8,128)S(1)}, f32[64,6,6,128]{3,0,2,1:T(8,128)}, u32[]{:S(2)}) copy-start(f32[64,6,6,128]{3,0,2,1:T(8,128)} %copy-done.8) | copy-start | bytes 3538948
  98.2 13.2 %copy-start.11 = (f32[64,6,6,128]{3,0,2,1:T(8,128)S(1)}, f32[64,6,6,128]{3,0,2,1:T(8,128)}, u32[]{:S(2)}) copy-start(f32[64,6,6,128]{3,0,2,1:T(8,128)} %copy-done.10) | copy-start | bytes 3538948
  98.2 16.9 %collective-permute-start.5 = (bf16[64,6,128]{2,0,1:T(8,128)(2,1)S(1)}, bf16[64,6,128]{2,0,1:T(8,128)(2,1)S(1)}, u32[]{:S(2)}, u32[]{:S(2)}) collective-permute-start(bf16[64,6,128]{2,0,1:T(8,128)(2,1)S(1)} %get-tuple-element.121), channel_id=1, source_target_pairs={{0,16},{16,32},{32,48},{1,17},{17,33},{33,49},{2,18},{18,34},{34,5... | collective-permute-start | bytes 294920 | tf_op jit(solution)/shard_map/ppermute | solution.py:24
  102.9 18.5 %collective-permute-start.6 = (f32[64,6,128]{2,1,0:T(8,128)}, f32[64,6,128]{2,1,0:T(8,128)}, u32[]{:S(2)}, u32[]{:S(2)}) collective-permute-start(f32[64,6,128]{2,1,0:T(8,128)} %get-tuple-element.111), channel_id=1, source_target_pairs={{1,0},{2,1},{3,2},{4,3},{5,4},{6,5},{7,6},{8,7},{9,8},{10,9},{11,1... | collective-permute-start | bytes 589832 | tf_op jit(solution)/shard_map/ppermute | solution.py:24
  104.2 19.0 %collective-permute-start.7 = (f32[64,6,128]{2,1,0:T(8,128)}, f32[64,6,128]{2,1,0:T(8,128)}, u32[]{:S(2)}, u32[]{:S(2)}) collective-permute-start(f32[64,6,128]{2,1,0:T(8,128)} %get-tuple-element.110), channel_id=1, source_target_pairs={{0,1},{1,2},{2,3},{3,4},{4,5},{5,6},{6,7},{7,8},{8,9},{9,10},{10,1... | collective-permute-start | bytes 589832 | tf_op jit(solution)/shard_map/ppermute | solution.py:24
  159.6 13.1 %copy-start.1 = (f32[64,6,6,128]{3,1,0,2:T(8,128)}, f32[64,6,6,128]{3,1,0,2:T(8,128)S(1)}, u32[]{:S(2)}) copy-start(f32[64,6,6,128]{3,1,0,2:T(8,128)S(1)} %get-tuple-element.106) | copy-start | bytes 3538948
  159.9 28.7 %collective-permute-start.8 = (f32[64,6,6,128]{3,0,2,1:T(8,128)S(1)}, f32[64,6,6,128]{3,0,2,1:T(8,128)S(1)}, u32[]{:S(2)}, u32[]{:S(2)}) collective-permute-start(f32[64,6,6,128]{3,0,2,1:T(8,128)S(1)} %copy.104), channel_id=1, source_target_pairs={{16,0},{32,16},{48,32},{17,1},{33,17},{49,33},{18,2},{34,18},{50,3... | collective-permute-start | bytes 3538952 | tf_op jit(solution)/shard_map/ppermute | solution.py:37
  161.2 31.0 %collective-permute-start.10 = (f32[64,6,6,128]{3,0,2,1:T(8,128)S(1)}, f32[64,6,6,128]{3,0,2,1:T(8,128)S(1)}, u32[]{:S(2)}, u32[]{:S(2)}) collective-permute-start(f32[64,6,6,128]{3,0,2,1:T(8,128)S(1)} %copy.104), channel_id=1, source_target_pairs={{1,0},{2,1},{3,2},{4,3},{5,4},{6,5},{7,6},{8,7},{9,8},{10,9},{11,1... | collective-permute-start | bytes 3538952 | tf_op jit(solution)/shard_map/ppermute | solution.py:37
  162.5 30.4 %collective-permute-start.11 = (f32[64,6,6,128]{3,0,2,1:T(8,128)S(1)}, f32[64,6,6,128]{3,0,2,1:T(8,128)S(1)}, u32[]{:S(2)}, u32[]{:S(2)}) collective-permute-start(f32[64,6,6,128]{3,0,2,1:T(8,128)S(1)} %copy.104), channel_id=1, source_target_pairs={{0,1},{1,2},{2,3},{3,4},{4,5},{5,6},{6,7},{7,8},{8,9},{9,10},{10,1... | collective-permute-start | bytes 3538952 | tf_op jit(solution)/shard_map/ppermute | solution.py:35
  167.1 28.0 %collective-permute-start.9 = (f32[64,6,6,128]{3,0,2,1:T(8,128)S(1)}, f32[64,6,6,128]{3,0,2,1:T(8,128)S(1)}, u32[]{:S(2)}, u32[]{:S(2)}) collective-permute-start(f32[64,6,6,128]{3,0,2,1:T(8,128)S(1)} %copy.104), channel_id=1, source_target_pairs={{0,16},{16,32},{32,48},{1,17},{17,33},{33,49},{2,18},{18,34},{34,5... | collective-permute-start | bytes 3538952 | tf_op jit(solution)/shard_map/ppermute | solution.py:35
  208.0 17.8 %collective-permute-start.12 = (bf16[64,6,128]{2,0,1:T(8,128)(2,1)S(1)}, bf16[64,6,128]{2,0,1:T(8,128)(2,1)S(1)}, u32[]{:S(2)}, u32[]{:S(2)}) collective-permute-start(bf16[64,6,128]{2,0,1:T(8,128)(2,1)S(1)} %get-tuple-element.120), channel_id=1, source_target_pairs={{16,0},{32,16},{48,32},{17,1},{33,17},{49,33},{18,2},{34,18},{50,3... | collective-permute-start | bytes 294920 | tf_op jit(solution)/shard_map/ppermute | solution.py:24
  210.3 11.7 %copy-start.13 = (f32[64,6,6,128]{3,0,2,1:T(8,128)S(1)}, f32[64,6,6,128]{3,0,2,1:T(8,128)}, u32[]{:S(2)}) copy-start(f32[64,6,6,128]{3,0,2,1:T(8,128)} %copy-done.12) | copy-start | bytes 3538948
  210.5 13.4 %copy-start.15 = (f32[64,6,6,128]{3,0,2,1:T(8,128)S(1)}, f32[64,6,6,128]{3,0,2,1:T(8,128)}, u32[]{:S(2)}) copy-start(f32[64,6,6,128]{3,0,2,1:T(8,128)} %copy-done.14) | copy-start | bytes 3538948
  210.5 17.2 %collective-permute-start.13 = (bf16[64,6,128]{2,0,1:T(8,128)(2,1)S(1)}, bf16[64,6,128]{2,0,1:T(8,128)(2,1)S(1)}, u32[]{:S(2)}, u32[]{:S(2)}) collective-permute-start(bf16[64,6,128]{2,0,1:T(8,128)(2,1)S(1)} %get-tuple-element.119), channel_id=1, source_target_pairs={{0,16},{16,32},{32,48},{1,17},{17,33},{33,49},{2,18},{18,34},{34,5... | collective-permute-start | bytes 294920 | tf_op jit(solution)/shard_map/ppermute | solution.py:24
  215.9 18.3 %collective-permute-start.14 = (f32[64,6,128]{2,1,0:T(8,128)}, f32[64,6,128]{2,1,0:T(8,128)S(1)}, u32[]{:S(2)}, u32[]{:S(2)}) collective-permute-start(f32[64,6,128]{2,1,0:T(8,128)} %get-tuple-element.109), channel_id=1, source_target_pairs={{1,0},{2,1},{3,2},{4,3},{5,4},{6,5},{7,6},{8,7},{9,8},{10,9},{11,1... | collective-permute-start | bytes 589832 | tf_op jit(solution)/shard_map/ppermute | solution.py:24
  217.2 18.7 %collective-permute-start.15 = (f32[64,6,128]{2,1,0:T(8,128)}, f32[64,6,128]{2,1,0:T(8,128)S(1)}, u32[]{:S(2)}, u32[]{:S(2)}) collective-permute-start(f32[64,6,128]{2,1,0:T(8,128)} %get-tuple-element.108), channel_id=1, source_target_pairs={{0,1},{1,2},{2,3},{3,4},{4,5},{5,6},{6,7},{7,8},{8,9},{9,10},{10,1... | collective-permute-start | bytes 589832 | tf_op jit(solution)/shard_map/ppermute | solution.py:24
  227.7 9.8 %copy-start.2 = (f32[64,6,6,128]{3,1,0,2:T(8,128)S(1)}, f32[64,6,6,128]{3,1,0,2:T(8,128)}, u32[]{:S(2)}) copy-start(f32[64,6,6,128]{3,1,0,2:T(8,128)} %copy-done.1) | copy-start | bytes 3538948
  227.7 9.8 %copy-start.4 = (f32[64,6,6,128]{3,0,2,1:T(8,128)S(1)}, f32[64,6,6,128]{3,0,2,1:T(8,128)}, u32[]{:S(2)}) copy-start(f32[64,6,6,128]{3,0,2,1:T(8,128)} %param.23) | copy-start | bytes 3538948
  254.9 118.3 %copy-start.7 = (f32[64,6,6,128]{3,1,0,2:T(8,128)S(1)}, f32[64,6,6,128]{3,1,0,2:T(8,128)}, u32[]{:S(2)}) copy-start(f32[64,6,6,128]{3,1,0,2:T(8,128)} %get-tuple-element.105) | copy-start | bytes 3538948
  254.9 118.3 %all-reduce.5.cloned.1.call-start = ((), (), s32[]{:S(2)}) async-start(), calls=%async_computation.1 | async-start | bytes 131072 | tf_op jit(solution)/shard_map/psum | solution.py:173
  323.4 199.6 %all-reduce.7.cloned.1.call-start = ((), (), s32[]{:S(2)}) async-start(), calls=%async_computation.2 | async-start | bytes 131072 | tf_op jit(solution)/shard_map/psum | solution.py:173
  (8 other events, 16.0 us)
Sparse Core Ops, SparseCore 0:
  255.0 64.9 all-gather.1
  323.5 49.6 all-reduce.4
  376.0 146.8 all-reduce.6
